TPU v7x, 32 devices: a whole 2x2x4 slice. The times are simulated.
32 devices in a mesh: groups: 2 (over x), row: 16 (over z, y, core).
Axes of the slice: x: 2, y: 2, z: 4, core: 2. Of those that a mesh axis runs over, the one named last changes fastest.
Arguments:
- base_grid: float32 [8192, 2048], P(('groups', 'row')), parts along dimension 0, may hold values from -6 to 6
- strip_minima: float32 [4096, 8, 128], P(('groups', 'row')), parts along dimension 0, may hold values from -6 to 6
- strip_owner: int32 [4096, 1], P(('groups', 'row')), parts along dimension 0, may hold values from 0 to 15; in each aligned block of 128 rows (0 to 127, 128 to 255, ...) at most 16 rows name the same one
- strip_cell: int32 [4096], P(('groups', 'row')), parts along dimension 0, may hold values from 0 to 511
Outputs:
- merged: float32 [8192, 2048], P(('groups', 'row')), parts along dimension 0
- opened_first: float32 [8192, 2048], P(('groups', 'row')), parts along dimension 0
- ground: float32 [8192, 2048], P(('groups', 'row')), parts along dimension 0
There are 2 independent parts, one for each index of `groups`. A program takes and returns all parts, laid end to end along the dimension named above; each array names one. Nothing has to cross between parts.
Inputs may be any that keep to these rules, and one draw needn't show every extreme that they name: `strip_owner`: among the strip blocks of one device no owner is named more than 16 times, a bound that some block reaches.
All inputs are finite; a program needn't handle non-finite values.
Results may differ from a plain program's by a relative error of at most 0.00002.
Values sent between devices are 32-bit elements; how exact they have to be, the bound alone decides.
A program may use at most 64 MiB of HBM per device.

v0:
```python
import jax
import jax.numpy as jnp
from jax import lax
from jax.sharding import PartitionSpec as P

BR = 8
BC = 128
HALF1 = 32
HALF2 = 64


def extended(cells, sides, width):
    for axis, dim in sides:
        count = lax.axis_size(axis)
        ends = count - 1
        head = lax.slice_in_dim(cells, 0, width, axis=dim)
        tail = lax.slice_in_dim(cells, cells.shape[dim] - width, cells.shape[dim], axis=dim)
        cells = jnp.concatenate(
            [
                lax.ppermute(tail, axis, [(i, (i + 1) % count) for i in range(ends)]),
                cells,
                lax.ppermute(head, axis, [((i + 1) % count, i) for i in range(ends)]),
            ],
            axis=dim,
        )
    return cells


def slide(values, half, axis, take_min):
    combine = jnp.minimum if take_min else jnp.maximum
    length = 2 * half + 1
    span = 1
    running = values
    while 2 * span <= length:
        size = running.shape[axis]
        running = combine(
            lax.slice_in_dim(running, 0, size - span, axis=axis),
            lax.slice_in_dim(running, span, size, axis=axis),
        )
        span = span * 2
    count = values.shape[axis] - length + 1
    return combine(
        lax.slice_in_dim(running, 0, count, axis=axis),
        lax.slice_in_dim(running, length - span, length - span + count, axis=axis),
    )


def columns(values, half, take_min):
    fill = jnp.inf if take_min else -jnp.inf
    padded = jnp.pad(values, ((0, 0), (half, half)), constant_values=fill)
    return slide(padded, half, 1, take_min)


def edge_fill(padded, width, fill):
    count = lax.axis_size("row")
    place = lax.axis_index("row")
    positions = jnp.arange(padded.shape[0])
    outside = (positions < width) & (place == 0) | (positions >= padded.shape[0] - width) & (
        place == count - 1
    )
    return jnp.where(outside[:, None], jnp.float32(fill), padded)


def near_rows(values, half):
    return extended(values, (("row", 0),), half)


def open_shallow(values, half):
    current = values
    for take_min in (True, False):
        fill = jnp.inf if take_min else -jnp.inf
        current = slide(edge_fill(near_rows(current, half), half, fill), half, 0, take_min)
        current = columns(current, half, take_min)
    return current


def opening(values, half):
    return open_shallow(values, half)


def on_device(base_grid, strip_minima, strip_owner, strip_cell):
    count = lax.axis_size("row")
    held = strip_minima.shape[0]
    capacity = max(2, 2 * held // count)
    owner = strip_owner[:, 0]
    hits = (owner[:, None] == jnp.arange(count, dtype=jnp.int32)[None, :]).astype(jnp.int32)
    slot = jnp.sum(jnp.cumsum(hits, axis=0) * hits, axis=1) - 1
    outbox = (
        jnp.full((count, capacity, BR, BC), jnp.inf, jnp.float32).at[owner, slot].set(strip_minima)
    )
    labels = jnp.zeros((count, capacity), jnp.int32).at[owner, slot].set(strip_cell)
    inbox, tags = (
        lax.all_to_all(outbox, "row", split_axis=0, concat_axis=0, tiled=True),
        lax.all_to_all(labels, "row", split_axis=0, concat_axis=0, tiled=True),
    )
    band_blocks = base_grid.shape[0] // BR
    col_blocks = base_grid.shape[1] // BC
    grid = base_grid.reshape(band_blocks, BR, col_blocks, BC)
    flat_tags = tags.reshape(-1)
    grid = grid.at[flat_tags // col_blocks, :, flat_tags % col_blocks, :].min(
        inbox.reshape(-1, BR, BC)
    )
    merged = grid.reshape(base_grid.shape)
    opened_first = opening(merged, HALF1)
    ground = opening(opened_first, HALF2)
    return (merged, opened_first, ground)


def solution(mesh):
    in_specs = (
        P(("groups", "row"), None),
        P(("groups", "row"), None, None),
        P(("groups", "row"), None),
        P(("groups", "row")),
    )
    out_specs = (P(("groups", "row"), None), P(("groups", "row"), None), P(("groups", "row"), None))
    return jax.shard_map(
        on_device, mesh=mesh, in_specs=in_specs, out_specs=out_specs, check_vma=False
    )
```

profile of v0, /device:TPU:14, one launch (start us, length us, event | category | flops | bytes accessed | tf_op | source)
XLA Modules:
  0.0 172.1 jit_solution(13336236612898530123)
XLA Ops:
  2.3 18.3 %scatter_fusion = s32[16,16]{1,0:T(8,128)} fusion(s32[16,16]{1,0:T(8,128)} %broadcast_in_dim.53, s32[128]{0:T(128)S(1)} %fusion.9, s32[128]{0:T(128)S(1)} %copy-done.5), kind=kCustom, calls=%fused_computation | custom fusion | bytes 2560 | tf_op jit(solution)/shard_map/scatter | solution.py:91
  20.6 6.4 %all-to-all-start = ((s32[16,1,16]{2,1,0:T(1,128)}), s32[16,1,16]{2,1,0:T(1,128)S(1)}, u32[]{:S(2)}, u32[]{:S(2)}) async-start(s32[16,1,16]{2,1,0:T(1,128)} %bitcast.6), calls=%async_computation | async-start | bytes 16384 | tf_op jit(solution)/shard_map/all_to_all | solution.py:94
  28.1 13.2 %scatter_fusion.1 = f32[16,16,8,128]{3,2,1,0:T(8,128)} fusion(f32[16,16,8,128]{3,2,1,0:T(8,128)} %broadcast_in_dim.54, s32[128]{0:T(128)S(1)} %fusion.9, f32[128,8,128]{2,1,0:T(8,128)S(1)} %copy-done.3), kind=kCustom, calls=%fused_computation.1 | custom fusion | bytes 1573888 | tf_op jit(solution)/shard_map/scatter | solution.py:89
  41.4 6.0 %all-to-all-start.1 = ((f32[16,16,8,128]{3,2,1,0:T(8,128)}), f32[16,16,8,128]{3,2,1,0:T(8,128)S(1)}, u32[]{:S(2)}, u32[]{:S(2)}) async-start(f32[16,16,8,128]{3,2,1,0:T(8,128)} %scatter_fusion.1), calls=%async_computation.1 | async-start | bytes 2097152 | tf_op jit(solution)/shard_map/all_to_all | solution.py:93
  48.7 23.4 %all-to-all-done.1 = f32[16,16,8,128]{3,2,1,0:T(8,128)S(1)} async-done(((f32[16,16,8,128]{3,2,1,0:T(8,128)}), f32[16,16,8,128]{3,2,1,0:T(8,128)S(1)}, u32[]{:S(2)}, u32[]{:S(2)}) %all-to-all-start.1) | async-done | bytes 1048608 | tf_op jit(solution)/shard_map/all_to_all | solution.py:93
  72.1 12.0 %scatter_fusion.2 = f32[32,8,16,128]{3,1,2,0:T(8,128)S(1)} fusion(f32[32,8,16,128]{3,1,2,0:T(8,128)S(1)} %bitcast.27, s32[256]{0:T(256)S(1)} %bitcast.24, f32[256,8,128]{2,1,0:T(8,128)S(1)} %bitcast.28), kind=kCustom, calls=%fused_computation.2 | custom fusion | flops 262144 | bytes 3147776 | tf_op jit(solution)/shard_map/scatter-min | solution.py:100
  84.2 1.9 %collective-permute-start = (f32[32,2048]{1,0:T(8,128)S(1)}, f32[32,2048]{1,0:T(8,128)S(1)}, u32[]{:S(2)}, u32[]{:S(2)}) collective-permute-start(f32[32,2048]{1,0:T(8,128)S(1)} %get-tuple-element.9), channel_id=1, source_target_pairs={{0,1},{1,2},{2,3},{3,4},{4,5},{5,6},{6,7},{7,8},{8,9},{9,10},{10,1... | collective-permute-start | bytes 786440 | tf_op jit(solution)/shard_map/ppermute | solution.py:20
  86.1 3.6 %collective-permute-start.1 = (f32[32,2048]{1,0:T(8,128)S(1)}, f32[32,2048]{1,0:T(8,128)S(1)}, u32[]{:S(2)}, u32[]{:S(2)}) collective-permute-start(f32[32,2048]{1,0:T(8,128)S(1)} %get-tuple-element.10), channel_id=1, source_target_pairs={{1,0},{2,1},{3,2},{4,3},{5,4},{6,5},{7,6},{8,7},{9,8},{10,9},{11,1... | collective-permute-start | bytes 786440 | tf_op jit(solution)/shard_map/ppermute | solution.py:22
  89.8 2.1 %collective-permute-done = f32[32,2048]{1,0:T(8,128)S(1)} collective-permute-done((f32[32,2048]{1,0:T(8,128)S(1)}, f32[32,2048]{1,0:T(8,128)S(1)}, u32[]{:S(2)}, u32[]{:S(2)}) %collective-permute-start) | collective-permute-done | bytes 262176 | tf_op jit(solution)/shard_map/ppermute | solution.py:20
  91.9 1.8 %collective-permute-done.1 = f32[32,2048]{1,0:T(8,128)S(1)} collective-permute-done((f32[32,2048]{1,0:T(8,128)S(1)}, f32[32,2048]{1,0:T(8,128)S(1)}, u32[]{:S(2)}, u32[]{:S(2)}) %collective-permute-start.1) | collective-permute-done | bytes 262176 | tf_op jit(solution)/shard_map/ppermute | solution.py:22
  96.2 1.2 slice_minimum_fusion.23
  101.6 4.5 %collective-permute-start.2 = (f32[32,2048]{1,0:T(8,128)S(1)}, f32[32,2048]{1,0:T(8,128)S(1)}, u32[]{:S(2)}, u32[]{:S(2)}) collective-permute-start(f32[32,2048]{1,0:T(8,128)S(1)} %get-tuple-element.7), channel_id=1, source_target_pairs={{0,1},{1,2},{2,3},{3,4},{4,5},{5,6},{6,7},{7,8},{8,9},{9,10},{10,1... | collective-permute-start | bytes 786440 | tf_op jit(solution)/shard_map/ppermute | solution.py:20
  106.0 2.1 %collective-permute-start.3 = (f32[32,2048]{1,0:T(8,128)S(1)}, f32[32,2048]{1,0:T(8,128)S(1)}, u32[]{:S(2)}, u32[]{:S(2)}) collective-permute-start(f32[32,2048]{1,0:T(8,128)S(1)} %get-tuple-element.8), channel_id=1, source_target_pairs={{1,0},{2,1},{3,2},{4,3},{5,4},{6,5},{7,6},{8,7},{9,8},{10,9},{11,1... | collective-permute-start | bytes 786440 | tf_op jit(solution)/shard_map/ppermute | solution.py:22
  108.2 1.3 collective-permute-done.2
  109.4 2.4 %collective-permute-done.3 = f32[32,2048]{1,0:T(8,128)S(1)} collective-permute-done((f32[32,2048]{1,0:T(8,128)S(1)}, f32[32,2048]{1,0:T(8,128)S(1)}, u32[]{:S(2)}, u32[]{:S(2)}) %collective-permute-start.3) | collective-permute-done | bytes 262176 | tf_op jit(solution)/shard_map/ppermute | solution.py:22
  119.8 4.7 %collective-permute-start.4 = (f32[64,2048]{1,0:T(8,128)S(1)}, f32[64,2048]{1,0:T(8,128)S(1)}, u32[]{:S(2)}, u32[]{:S(2)}) collective-permute-start(f32[64,2048]{1,0:T(8,128)S(1)} %get-tuple-element.5), channel_id=1, source_target_pairs={{0,1},{1,2},{2,3},{3,4},{4,5},{5,6},{6,7},{7,8},{8,9},{9,10},{10,1... | collective-permute-start | bytes 1572872 | tf_op jit(solution)/shard_map/ppermute | solution.py:20
  124.6 2.1 %collective-permute-start.5 = (f32[64,2048]{1,0:T(8,128)S(1)}, f32[64,2048]{1,0:T(8,128)S(1)}, u32[]{:S(2)}, u32[]{:S(2)}) collective-permute-start(f32[64,2048]{1,0:T(8,128)S(1)} %get-tuple-element.6), channel_id=1, source_target_pairs={{1,0},{2,1},{3,2},{4,3},{5,4},{6,5},{7,6},{8,7},{9,8},{10,9},{11,1... | collective-permute-start | bytes 1572872 | tf_op jit(solution)/shard_map/ppermute | solution.py:22
  126.7 3.8 %collective-permute-done.4 = f32[64,2048]{1,0:T(8,128)S(1)} collective-permute-done((f32[64,2048]{1,0:T(8,128)S(1)}, f32[64,2048]{1,0:T(8,128)S(1)}, u32[]{:S(2)}, u32[]{:S(2)}) %collective-permute-start.4) | collective-permute-done | bytes 524320 | tf_op jit(solution)/shard_map/ppermute | solution.py:20
  130.5 5.1 %collective-permute-done.5 = f32[64,2048]{1,0:T(8,128)S(1)} collective-permute-done((f32[64,2048]{1,0:T(8,128)S(1)}, f32[64,2048]{1,0:T(8,128)S(1)}, u32[]{:S(2)}, u32[]{:S(2)}) %collective-permute-start.5) | collective-permute-done | bytes 524320 | tf_op jit(solution)/shard_map/ppermute | solution.py:22
  139.0 1.2 slice_minimum_fusion.22
  145.1 2.3 %collective-permute-start.6 = (f32[64,2048]{1,0:T(8,128)S(1)}, f32[64,2048]{1,0:T(8,128)S(1)}, u32[]{:S(2)}, u32[]{:S(2)}) collective-permute-start(f32[64,2048]{1,0:T(8,128)S(1)} %get-tuple-element.3), channel_id=1, source_target_pairs={{0,1},{1,2},{2,3},{3,4},{4,5},{5,6},{6,7},{7,8},{8,9},{9,10},{10,1... | collective-permute-start | bytes 1572872 | tf_op jit(solution)/shard_map/ppermute | solution.py:20
  147.4 3.7 %collective-permute-start.7 = (f32[64,2048]{1,0:T(8,128)S(1)}, f32[64,2048]{1,0:T(8,128)S(1)}, u32[]{:S(2)}, u32[]{:S(2)}) collective-permute-start(f32[64,2048]{1,0:T(8,128)S(1)} %get-tuple-element.4), channel_id=1, source_target_pairs={{1,0},{2,1},{3,2},{4,3},{5,4},{6,5},{7,6},{8,7},{9,8},{10,9},{11,1... | collective-permute-start | bytes 1572872 | tf_op jit(solution)/shard_map/ppermute | solution.py:22
  151.1 10.3 %collective-permute-done.6 = f32[64,2048]{1,0:T(8,128)S(1)} collective-permute-done((f32[64,2048]{1,0:T(8,128)S(1)}, f32[64,2048]{1,0:T(8,128)S(1)}, u32[]{:S(2)}, u32[]{:S(2)}) %collective-permute-start.6) | collective-permute-done | bytes 524320 | tf_op jit(solution)/shard_map/ppermute | solution.py:20
  170.1 1.9 %slice_maximum_fusion.26 = f32[256,2048]{1,0:T(8,128)} fusion(f32[256,2049]{1,0:T(8,128)S(1)} %slice_maximum_fusion.11), kind=kLoop, calls=%fused_computation.59 | loop fusion | flops 524288 | bytes 6291456 | tf_op jit(solution)/shard_map/max | solution.py:42
  (91 shorter events, 35.3 us)
Async XLA Ops:
  0.6 0.7 copy-start.4
  0.6 1.7 copy-start.5
  0.7 27.5 %copy-start.3 = (f32[128,8,128]{2,1,0:T(8,128)S(1)}, f32[128,8,128]{2,1,0:T(8,128)}, u32[]{:S(2)}) copy-start(f32[128,8,128]{2,1,0:T(8,128)} %param.5) | copy-start | bytes 1572868
  20.6 20.7 %all-to-all-start = ((s32[16,1,16]{2,1,0:T(1,128)}), s32[16,1,16]{2,1,0:T(1,128)S(1)}, u32[]{:S(2)}, u32[]{:S(2)}) async-start(s32[16,1,16]{2,1,0:T(1,128)} %bitcast.6), calls=%async_computation | async-start | bytes 16384 | tf_op jit(solution)/shard_map/all_to_all | solution.py:94
  27.0 45.1 %copy-start.1 = (f32[256,2048]{1,0:T(8,128)S(1)}, f32[256,2048]{1,0:T(8,128)}, u32[]{:S(2)}) copy-start(f32[256,2048]{1,0:T(8,128)} %param.4) | copy-start | bytes 6291460
  41.4 30.7 %all-to-all-start.1 = ((f32[16,16,8,128]{3,2,1,0:T(8,128)}), f32[16,16,8,128]{3,2,1,0:T(8,128)S(1)}, u32[]{:S(2)}, u32[]{:S(2)}) async-start(f32[16,16,8,128]{3,2,1,0:T(8,128)} %scatter_fusion.1), calls=%async_computation.1 | async-start | bytes 2097152 | tf_op jit(solution)/shard_map/all_to_all | solution.py:93
  84.1 9.8 %copy-start = (f32[32,8,16,128]{3,1,2,0:T(8,128)}, f32[32,8,16,128]{3,1,2,0:T(8,128)S(1)}, u32[]{:S(2)}) copy-start(f32[32,8,16,128]{3,1,2,0:T(8,128)S(1)} %scatter_fusion.2) | copy-start | bytes 6291460
  84.2 7.7 %collective-permute-start = (f32[32,2048]{1,0:T(8,128)S(1)}, f32[32,2048]{1,0:T(8,128)S(1)}, u32[]{:S(2)}, u32[]{:S(2)}) collective-permute-start(f32[32,2048]{1,0:T(8,128)S(1)} %get-tuple-element.9), channel_id=1, source_target_pairs={{0,1},{1,2},{2,3},{3,4},{4,5},{5,6},{6,7},{7,8},{8,9},{9,10},{10,1... | collective-permute-start | bytes 786440 | tf_op jit(solution)/shard_map/ppermute | solution.py:20
  86.1 7.5 %collective-permute-start.1 = (f32[32,2048]{1,0:T(8,128)S(1)}, f32[32,2048]{1,0:T(8,128)S(1)}, u32[]{:S(2)}, u32[]{:S(2)}) collective-permute-start(f32[32,2048]{1,0:T(8,128)S(1)} %get-tuple-element.10), channel_id=1, source_target_pairs={{1,0},{2,1},{3,2},{4,3},{5,4},{6,5},{7,6},{8,7},{9,8},{10,9},{11,1... | collective-permute-start | bytes 786440 | tf_op jit(solution)/shard_map/ppermute | solution.py:22
  101.6 7.9 %collective-permute-start.2 = (f32[32,2048]{1,0:T(8,128)S(1)}, f32[32,2048]{1,0:T(8,128)S(1)}, u32[]{:S(2)}, u32[]{:S(2)}) collective-permute-start(f32[32,2048]{1,0:T(8,128)S(1)} %get-tuple-element.7), channel_id=1, source_target_pairs={{0,1},{1,2},{2,3},{3,4},{4,5},{5,6},{6,7},{7,8},{8,9},{9,10},{10,1... | collective-permute-start | bytes 786440 | tf_op jit(solution)/shard_map/ppermute | solution.py:20
  106.0 5.8 %collective-permute-start.3 = (f32[32,2048]{1,0:T(8,128)S(1)}, f32[32,2048]{1,0:T(8,128)S(1)}, u32[]{:S(2)}, u32[]{:S(2)}) collective-permute-start(f32[32,2048]{1,0:T(8,128)S(1)} %get-tuple-element.8), channel_id=1, source_target_pairs={{1,0},{2,1},{3,2},{4,3},{5,4},{6,5},{7,6},{8,7},{9,8},{10,9},{11,1... | collective-permute-start | bytes 786440 | tf_op jit(solution)/shard_map/ppermute | solution.py:22
  119.7 16.1 %copy-start.2 = (f32[256,2048]{1,0:T(8,128)}, f32[256,2048]{1,0:T(8,128)S(1)}, u32[]{:S(2)}) copy-start(f32[256,2048]{1,0:T(8,128)S(1)} %slice_maximum_fusion.28) | copy-start | bytes 6291460
  119.8 10.7 %collective-permute-start.4 = (f32[64,2048]{1,0:T(8,128)S(1)}, f32[64,2048]{1,0:T(8,128)S(1)}, u32[]{:S(2)}, u32[]{:S(2)}) collective-permute-start(f32[64,2048]{1,0:T(8,128)S(1)} %get-tuple-element.5), channel_id=1, source_target_pairs={{0,1},{1,2},{2,3},{3,4},{4,5},{5,6},{6,7},{7,8},{8,9},{9,10},{10,1... | collective-permute-start | bytes 1572872 | tf_op jit(solution)/shard_map/ppermute | solution.py:20
  124.6 11.0 %collective-permute-start.5 = (f32[64,2048]{1,0:T(8,128)S(1)}, f32[64,2048]{1,0:T(8,128)S(1)}, u32[]{:S(2)}, u32[]{:S(2)}) collective-permute-start(f32[64,2048]{1,0:T(8,128)S(1)} %get-tuple-element.6), channel_id=1, source_target_pairs={{1,0},{2,1},{3,2},{4,3},{5,4},{6,5},{7,6},{8,7},{9,8},{10,9},{11,1... | collective-permute-start | bytes 1572872 | tf_op jit(solution)/shard_map/ppermute | solution.py:22
  145.1 16.3 %collective-permute-start.6 = (f32[64,2048]{1,0:T(8,128)S(1)}, f32[64,2048]{1,0:T(8,128)S(1)}, u32[]{:S(2)}, u32[]{:S(2)}) collective-permute-start(f32[64,2048]{1,0:T(8,128)S(1)} %get-tuple-element.3), channel_id=1, source_target_pairs={{0,1},{1,2},{2,3},{3,4},{4,5},{5,6},{6,7},{7,8},{8,9},{9,10},{10,1... | collective-permute-start | bytes 1572872 | tf_op jit(solution)/shard_map/ppermute | solution.py:20
  147.4 14.0 %collective-permute-start.7 = (f32[64,2048]{1,0:T(8,128)S(1)}, f32[64,2048]{1,0:T(8,128)S(1)}, u32[]{:S(2)}, u32[]{:S(2)}) collective-permute-start(f32[64,2048]{1,0:T(8,128)S(1)} %get-tuple-element.4), channel_id=1, source_target_pairs={{1,0},{2,1},{3,2},{4,3},{5,4},{6,5},{7,6},{8,7},{9,8},{10,9},{11,1... | collective-permute-start | bytes 1572872 | tf_op jit(solution)/shard_map/ppermute | solution.py:22
where the time goes:
time: 174 us; the launch traced here: 172 us
  waiting for transfers between devices  50.1 us (29%)
  other arithmetic  48.5 us (28%)
  starting transfers between devices  37.4 us (21%)
  local copies, waits for them, and re-layouts  34.7 us (20%)
    all_to_all x1, waiting for transfers between devices, on_device(): lax.all_to_all(outbox, 'row', split_axis=0, concat_axis=0, tiled=True)  23.4 us
    scatter x1, local copies, waits for them, and re-layouts, on_device(): jnp.zeros((count, capacity), jnp.int32).at[owner, slot].set(strip_cell)  18.3 us
    ppermute x4, waiting for transfers between devices, extended(): lax.ppermute(tail, axis, [(i, (i + 1) % count) for i in range(ends)])  17.4 us
    min x26, other arithmetic, slide(): combine(lax.slice_in_dim(running, 0, size - span, axis=axis), lax.slice_i...  14.6 us
    max x26, other arithmetic, slide(): combine(lax.slice_in_dim(running, 0, size - span, axis=axis), lax.slice_i...  14.6 us
    ppermute x4, starting transfers between devices, extended(): lax.ppermute(tail, axis, [(i, (i + 1) % count) for i in range(ends)])  13.4 us
    scatter x1, local copies, waits for them, and re-layouts, on_device(): jnp.full((count, capacity, BR, BC), jnp.inf, jnp.float32).at[owner, slot]  13.2 us
    another operation x1, other arithmetic, on_device(): grid.at[flat_tags // col_blocks, :, flat_tags % col_blocks, :]  12 us
  transfers between devices with their start and end apart: 10, of which 8 were waited for; matrix products, arithmetic and copies ran while one was open for 9% of the time, Pallas kernels for 0%

commit v1 on v0

v1 whole, which is shorter than its diff:
```python
import functools

import jax
import jax.numpy as jnp
from jax import lax
from jax.experimental import pallas as pl
from jax.experimental.pallas import tpu as pltpu
from jax.sharding import PartitionSpec as P

BR = 8
BC = 128
HALF1 = 32
HALF2 = 64
MESH = pl.DeviceIdType.MESH
VMEM_LIMIT = 48 * 1024 * 1024


def pack_kernel(count, capacity, held, owner_ref, cell_ref, strips_ref, box_ref, used_ref):
    lane = lax.broadcasted_iota(jnp.int32, (1, BC), 1)

    def clear(i, c):
        used_ref[i] = 0
        box_ref[i, capacity] = jnp.full((BR, BC), -1.0, jnp.float32)
        return c

    lax.fori_loop(0, count, clear, 0)

    def place(k, c):
        owner = owner_ref[k]
        slot = used_ref[owner]
        used_ref[owner] = slot + 1
        box_ref[owner, slot] = strips_ref[k]
        tags = box_ref[owner, capacity, 0:1, :]
        box_ref[owner, capacity, 0:1, :] = jnp.where(
            lane == slot, cell_ref[k].astype(jnp.float32), tags
        )
        return c

    lax.fori_loop(0, held, place, 0)


def merge_kernel(entries, capacity, col_blocks, tags_ref, base_ref, box_ref, out_ref):
    out_ref[...] = base_ref[...]

    def place(e, c):
        tag = tags_ref[e]

        @pl.when(tag >= 0)
        def _():
            row = pl.multiple_of((tag // col_blocks) * BR, BR)
            col = pl.multiple_of((tag % col_blocks) * BC, BC)
            here = (pl.ds(row, BR), pl.ds(col, BC))
            out_ref[here] = jnp.minimum(out_ref[here], box_ref[e // capacity, e % capacity])

        return c

    lax.fori_loop(0, entries, place, 0)


def across(x, half, take_min):
    combine = jnp.minimum if take_min else jnp.maximum
    fill = jnp.inf if take_min else -jnp.inf
    cols = x.shape[1]
    run = jnp.concatenate([x, jnp.full((x.shape[0], BC), fill, jnp.float32)], axis=1)
    width = cols + BC
    span = 1
    while span < half:
        run = combine(run, pltpu.roll(run, width - span, axis=1))
        span *= 2
    run = combine(run, pltpu.roll(run, half, axis=1))
    run = combine(run, pltpu.roll(run, width - 1, axis=1))
    return run[:, :cols]


def down(x, half, take_min):
    combine = jnp.minimum if take_min else jnp.maximum
    rows = x.shape[0]
    run = x
    span = 1
    while span < 8:
        run = combine(run, pltpu.roll(run, rows - span, axis=0))
        span *= 2
    while span < 2 * half:
        size = run.shape[0]
        run = combine(run[: size - span], run[span:])
        span *= 2
    keep = rows - 2 * half
    return combine(run[:keep], x[2 * half :])


def open_rows(src, first, out, dst, dst_first, half, is_top, is_bottom):
    def body(c, carry):
        cols = pl.ds(pl.multiple_of(c * BC, BC), BC)
        low = down(src[first : first + out + 4 * half, cols], half, True)
        parts = [low[:half], low[half : half + out], low[half + out :]]
        if is_top is not None:
            parts[0] = jnp.where(is_top, -jnp.inf, parts[0])
        if is_bottom is not None:
            parts[2] = jnp.where(is_bottom, -jnp.inf, parts[2])
        dst[dst_first : dst_first + out, cols] = down(jnp.concatenate(parts, axis=0), half, False)
        return carry

    lax.fori_loop(0, src.shape[1] // BC, body, 0)


def row_blocks(first, rows, body):
    def step(i, c):
        body(pl.multiple_of(first + i * 8, 8))
        return c

    lax.fori_loop(0, rows // 8, step, 0)


def open_kernel(n, m_ref, first_ref, ground_ref, near, far, mid, send_sem, recv_sem):
    place = lax.axis_index("row")
    rows = m_ref.shape[0]
    is_top, is_bottom = place == 0, place == n - 1
    edge1, edge2 = 2 * HALF1, 2 * HALF2

    barrier = pltpu.get_barrier_semaphore()

    @pl.when(place > 0)
    def _():
        pl.semaphore_signal(barrier, inc=1, device_id={"row": place - 1}, device_id_type=MESH)

    @pl.when(place < n - 1)
    def _():
        pl.semaphore_signal(barrier, inc=1, device_id={"row": place + 1}, device_id_type=MESH)

    pl.semaphore_wait(barrier, jnp.where(is_top | is_bottom, 1, 2))

    def up(buf, src, dst, size, at):
        return pltpu.make_async_remote_copy(
            src_ref=buf.at[pl.ds(src, size)],
            dst_ref=buf.at[pl.ds(dst, size)],
            send_sem=send_sem.at[at],
            recv_sem=recv_sem.at[at],
            device_id={"row": place - 1},
            device_id_type=MESH,
        )

    def down_to(buf, src, dst, size, at):
        return pltpu.make_async_remote_copy(
            src_ref=buf.at[pl.ds(src, size)],
            dst_ref=buf.at[pl.ds(dst, size)],
            send_sem=send_sem.at[at],
            recv_sem=recv_sem.at[at],
            device_id={"row": place + 1},
            device_id_type=MESH,
        )

    plans = [
        (near, (edge1, edge1 + rows, edge1), (rows, 0, edge1)),
        (far, (edge2 + 64, edge2 + rows + 64, 64), (edge2 + 128, 0, 64)),
        (far, (edge2, edge2 + rows, 64), (edge2 + 192, 64, 64)),
    ]

    def start(i):
        buf, u, d = plans[i]

        @pl.when(place > 0)
        def _():
            up(buf, *u, 2 * i).start()

        @pl.when(place < n - 1)
        def _():
            down_to(buf, *d, 2 * i + 1).start()

    def receive(i):
        buf, u, d = plans[i]

        @pl.when(place < n - 1)
        def _():
            up(buf, *u, 2 * i).wait_recv()

        @pl.when(place > 0)
        def _():
            down_to(buf, *d, 2 * i + 1).wait_recv()

    def sent(i):
        buf, u, d = plans[i]

        @pl.when(place > 0)
        def _():
            up(buf, *u, 2 * i).wait_send()

        @pl.when(place < n - 1)
        def _():
            down_to(buf, *d, 2 * i + 1).wait_send()

    def narrow(r):
        near[pl.ds(r + edge1, 8), :] = across(m_ref[pl.ds(r, 8), :], HALF1, True)

    def finish_first(r):
        y = across(mid[pl.ds(r, 8), :], HALF1, False)
        first_ref[pl.ds(r, 8), :] = y
        far[pl.ds(r + edge2, 8), :] = across(y, HALF2, True)

    row_blocks(0, 64, narrow)
    row_blocks(rows - 64, 64, narrow)
    start(0)

    @pl.when(is_top)
    def _():
        near[0:edge1, :] = jnp.full((edge1, near.shape[1]), jnp.inf, jnp.float32)
        far[0:edge2, :] = jnp.full((edge2, far.shape[1]), jnp.inf, jnp.float32)

    @pl.when(is_bottom)
    def _():
        near[edge1 + rows :, :] = jnp.full((edge1, near.shape[1]), jnp.inf, jnp.float32)
        far[edge2 + rows :, :] = jnp.full((edge2, far.shape[1]), jnp.inf, jnp.float32)

    row_blocks(64, rows - 128, narrow)
    open_rows(near, edge1, rows - 128, mid, 64, HALF1, None, None)
    row_blocks(64, rows - 128, finish_first)
    start(1)
    receive(0)
    open_rows(near, 0, 64, mid, 0, HALF1, is_top, None)
    open_rows(near, rows - 64, 64, mid, rows - 64, HALF1, None, is_bottom)
    row_blocks(0, 64, finish_first)
    row_blocks(rows - 64, 64, finish_first)
    start(2)
    receive(1)
    receive(2)
    open_rows(far, 0, rows, mid, 0, HALF2, is_top, is_bottom)

    def finish_ground(r):
        ground_ref[pl.ds(r, 8), :] = across(mid[pl.ds(r, 8), :], HALF2, False)

    row_blocks(0, rows, finish_ground)
    for i in range(3):
        sent(i)


def on_device(n, base_grid, strip_minima, strip_owner, strip_cell):
    held = strip_minima.shape[0]
    capacity = max(2, 2 * held // n)
    rows, cols = base_grid.shape
    vmem = pl.BlockSpec(memory_space=pltpu.VMEM)
    smem = pl.BlockSpec(memory_space=pltpu.SMEM)
    outbox = pl.pallas_call(
        functools.partial(pack_kernel, n, capacity, held),
        out_shape=jax.ShapeDtypeStruct((n, capacity + 1, BR, BC), jnp.float32),
        in_specs=[smem, smem, vmem],
        out_specs=vmem,
        scratch_shapes=[pltpu.SMEM((n,), jnp.int32)],
        compiler_params=pltpu.CompilerParams(vmem_limit_bytes=VMEM_LIMIT),
        name="pack",
    )(strip_owner[:, 0], strip_cell, strip_minima)
    inbox = lax.all_to_all(outbox, "row", split_axis=0, concat_axis=0, tiled=True)
    tags = inbox[:, capacity, 0, :capacity].astype(jnp.int32).reshape(-1)
    merged = pl.pallas_call(
        functools.partial(merge_kernel, n * capacity, capacity, cols // BC),
        out_shape=jax.ShapeDtypeStruct((rows, cols), jnp.float32),
        in_specs=[smem, vmem, vmem],
        out_specs=vmem,
        compiler_params=pltpu.CompilerParams(vmem_limit_bytes=VMEM_LIMIT),
        name="merge",
    )(tags, base_grid, inbox)
    shape = jax.ShapeDtypeStruct((rows, cols), jnp.float32)
    opened_first, ground = pl.pallas_call(
        functools.partial(open_kernel, n),
        out_shape=(shape, shape),
        in_specs=[vmem],
        out_specs=(vmem, vmem),
        scratch_shapes=[
            pltpu.VMEM((rows + 4 * HALF1, cols), jnp.float32),
            pltpu.VMEM((rows + 4 * HALF2, cols), jnp.float32),
            pltpu.VMEM((rows, cols), jnp.float32),
            pltpu.SemaphoreType.DMA((6,)),
            pltpu.SemaphoreType.DMA((6,)),
        ],
        compiler_params=pltpu.CompilerParams(
            collective_id=0, has_side_effects=True, vmem_limit_bytes=VMEM_LIMIT
        ),
        name="opening",
    )(merged)
    return (merged, opened_first, ground)


def solution(mesh):
    in_specs = (
        P(("groups", "row"), None),
        P(("groups", "row"), None, None),
        P(("groups", "row"), None),
        P(("groups", "row")),
    )
    out_specs = (P(("groups", "row"), None), P(("groups", "row"), None), P(("groups", "row"), None))
    return jax.shard_map(
        functools.partial(on_device, mesh.shape["row"]),
        mesh=mesh,
        in_specs=in_specs,
        out_specs=out_specs,
        check_vma=False,
    )
```

time: 174 us -> 146 us (0.84)
  Pallas kernels: 0 us -> 106 us
  waiting for transfers between devices: 50.1 us -> 0 us
  other arithmetic: 48.5 us -> 0.03 us
  starting transfers between devices: 37.4 us -> 0 us
  blocking collectives: 0 us -> 32.4 us
  local copies, waits for them, and re-layouts: 34.7 us -> 5.22 us
    pallas_call x0 -> x3, Pallas kernels: none -> 106 us  [the longest x1 95.9 us: on_device(): pl.pallas_call(functools.partial(open_kernel, n), out_shape=(shape, shape...]
    all_to_all x0 -> x1, blocking collectives: none -> 32.4 us  [on_device(): lax.all_to_all(outbox, 'row', split_axis=0, concat_axis=0, tiled=True)]
    scatter x2 -> x0, local copies, waits for them, and re-layouts: 31.5 us -> none  [the longest x1 18.3 us: on_device(): jnp.zeros((count, capacity), jnp.int32).at[owner, slot].set(strip_cell)]
    ppermute x8 -> x0, waiting for transfers between devices: 26.7 us -> none  [the longest x4 17.4 us: extended(): lax.ppermute(tail, axis, [(i, (i + 1) % count) for i in range(ends)])]
    ppermute x8 -> x0, starting transfers between devices: 25 us -> none  [the longest x4 13.4 us: extended(): lax.ppermute(tail, axis, [(i, (i + 1) % count) for i in range(ends)])]
    all_to_all x2 -> x0, waiting for transfers between devices: 23.4 us -> none  [the longest x1 23.4 us: on_device(): lax.all_to_all(outbox, 'row', split_axis=0, concat_axis=0, tiled=True)]
    max x30 -> x0, other arithmetic: 17.8 us -> none  [the longest x26 14.6 us: slide(): combine(lax.slice_in_dim(running, 0, size - span, axis=axis), lax.slice_i...]
    min x30 -> x0, other arithmetic: 16.5 us -> none  [the longest x26 14.6 us: slide(): combine(lax.slice_in_dim(running, 0, size - span, axis=axis), lax.slice_i...]
  transfers between devices with their start and end apart: 10 -> 0, of which waited for: 8 -> 0; matrix products, arithmetic and copies ran while one was open for 9% -> 0% of each run, Pallas kernels for 0% -> 0%
where the time goes in v1:
time: 146 us; the launch traced here: 145 us
  Pallas kernels  106 us (73%)
  blocking collectives  32.4 us (22%)
  local copies, waits for them, and re-layouts  5.22 us (4%)
    pallas_call x1, Pallas kernels, on_device(): pl.pallas_call(functools.partial(open_kernel, n), out_shape=(shape, shape...  95.9 us
    all_to_all x1, blocking collectives, on_device(): lax.all_to_all(outbox, 'row', split_axis=0, concat_axis=0, tiled=True)  32.4 us
    pallas_call x1, Pallas kernels, on_device(): pl.pallas_call(functools.partial(merge_kernel, n * capacity, capacity, co...  8.41 us
    unnamed x10, local copies, waits for them, and re-layouts  5.14 us

profile of v1, /device:TPU:14, one launch (start us, length us, event | category | flops | bytes accessed | tf_op | source)
XLA Modules:
  0.0 144.8 jit_solution(17849006659249206181)
XLA Ops:
  0.6 0.0 copy-start
  0.6 0.0 copy-start.1
  0.7 1.2 copy-done.1
  1.8 0.0 copy-start.2
  1.8 0.7 copy-done.2
  2.5 0.0 copy-start.3
  2.5 0.7 copy-done.3
  3.1 2.2 %pack.1 = f32[16,17,8,128]{3,2,1,0:T(8,128)S(1)} custom-call(s32[128]{0:T(128)S(1)} %bitcast.1, s32[128]{0:T(128)S(1)} %copy-done.3, f32[128,8,128]{2,1,0:T(8,128)S(1)} %copy-done.1), custom_call_target="tpu_custom_call" | custom-call | tf_op jit(solution)/shard_map/pack/pallas_call | solution.py:241
  5.4 32.4 %all_to_all.5.box_ref = f32[16,17,8,128]{3,2,1,0:T(8,128)S(1)} all-to-all(f32[16,17,8,128]{3,2,1,0:T(8,128)S(1)} %pack.1), channel_id=1, replica_groups=mesh['groups'=2,'row'=16] {'row'}, dimensions={0} | all-to-all | bytes 2228224 | tf_op jit(solution)/shard_map/all_to_all | solution.py:250
  37.8 0.1 convert_element_type.8.tags_ref
  37.9 0.0 copy-done
  37.9 8.4 %merge.1.m_ref = f32[256,2048]{1,0:T(8,128)} custom-call(s32[256]{0:T(256)S(1)} %convert_element_type.8.tags_ref, f32[256,2048]{1,0:T(8,128)S(1)} %copy-done, f32[16,17,8,128]{3,2,1,0:T(8,128)S(1)} %all_to_all.5.box_ref), custom_call_target="tpu_custom_call" | custom-call | tf_op jit(solution)/shard_map/merge/pallas_call | solution.py:252
  46.3 95.9 %opening.1 = (f32[256,2048]{1,0:T(8,128)S(1)}, f32[256,2048]{1,0:T(8,128)S(1)}) custom-call(f32[256,2048]{1,0:T(8,128)} %merge.1.m_ref), custom_call_target="tpu_custom_call" | custom-call | tf_op jit(solution)/shard_map/opening/pallas_call | solution.py:261
  142.2 1.3 copy.9
  143.5 1.3 copy.10
  (1 shorter events, 0.0 us)
Async XLA Ops:
  0.6 37.3 %copy-start = (f32[256,2048]{1,0:T(8,128)S(1)}, f32[256,2048]{1,0:T(8,128)}, u32[]{:S(2)}) copy-start(f32[256,2048]{1,0:T(8,128)} %base_ref.1) | copy-start | bytes 6291460
  0.6 1.2 copy-start.1
  1.8 0.7 copy-start.2
  2.5 0.7 copy-start.3

commit v2 on v1

--- a/solution.py
+++ b/solution.py
@@ -11,6 +11,7 @@
 BC = 128
 HALF1 = 32
 HALF2 = 64
+TALL = 64
 MESH = pl.DeviceIdType.MESH
 VMEM_LIMIT = 48 * 1024 * 1024
 
@@ -105,10 +106,10 @@
 
 def row_blocks(first, rows, body):
     def step(i, c):
-        body(pl.multiple_of(first + i * 8, 8))
-        return c
-
-    lax.fori_loop(0, rows // 8, step, 0)
+        body(pl.multiple_of(first + i * TALL, TALL))
+        return c
+
+    lax.fori_loop(0, rows // TALL, step, 0)
 
 
 def open_kernel(n, m_ref, first_ref, ground_ref, near, far, mid, send_sem, recv_sem):
@@ -189,12 +190,12 @@
             down_to(buf, *d, 2 * i + 1).wait_send()
 
     def narrow(r):
-        near[pl.ds(r + edge1, 8), :] = across(m_ref[pl.ds(r, 8), :], HALF1, True)
+        near[pl.ds(r + edge1, TALL), :] = across(m_ref[pl.ds(r, TALL), :], HALF1, True)
 
     def finish_first(r):
-        y = across(mid[pl.ds(r, 8), :], HALF1, False)
-        first_ref[pl.ds(r, 8), :] = y
-        far[pl.ds(r + edge2, 8), :] = across(y, HALF2, True)
+        y = across(mid[pl.ds(r, TALL), :], HALF1, False)
+        first_ref[pl.ds(r, TALL), :] = y
+        far[pl.ds(r + edge2, TALL), :] = across(y, HALF2, True)
 
     row_blocks(0, 64, narrow)
     row_blocks(rows - 64, 64, narrow)
@@ -225,7 +226,7 @@
     open_rows(far, 0, rows, mid, 0, HALF2, is_top, is_bottom)
 
     def finish_ground(r):
-        ground_ref[pl.ds(r, 8), :] = across(mid[pl.ds(r, 8), :], HALF2, False)
+        ground_ref[pl.ds(r, TALL), :] = across(mid[pl.ds(r, TALL), :], HALF2, False)
 
     row_blocks(0, rows, finish_ground)
     for i in range(3):

time: 146 us -> 104 us (0.71)
  Pallas kernels: 106 us -> 63.9 us
    pallas_call x1, Pallas kernels: 95.9 us -> 53.9 us  [on_device(): pl.pallas_call(functools.partial(open_kernel, n), out_shape=(shape, shape...]
where the time goes in v2:
time: 104 us; the launch traced here: 102 us
  Pallas kernels  63.9 us (61%)
  blocking collectives  32.4 us (31%)
  local copies, waits for them, and re-layouts  5.22 us (5%)
    pallas_call x1, Pallas kernels, on_device(): pl.pallas_call(functools.partial(open_kernel, n), out_shape=(shape, shape...  53.9 us
    all_to_all x1, blocking collectives, on_device(): lax.all_to_all(outbox, 'row', split_axis=0, concat_axis=0, tiled=True)  32.4 us
    pallas_call x1, Pallas kernels, on_device(): pl.pallas_call(functools.partial(merge_kernel, n * capacity, capacity, co...  7.73 us
    unnamed x10, local copies, waits for them, and re-layouts  5.14 us
    pallas_call x1, Pallas kernels, on_device(): pl.pallas_call(functools.partial(pack_kernel, n, capacity, held), out_sha...  2.2 us

profile of v2, /device:TPU:14, one launch (start us, length us, event | category | flops | bytes accessed | tf_op | source)
XLA Modules:
  0.0 102.2 jit_solution(13868726159449495261)
XLA Ops:
  0.6 0.0 copy-start
  0.6 0.0 copy-start.1
  0.7 1.2 %copy-done.1 = f32[128,8,128]{2,1,0:T(8,128)S(1)} copy-done((f32[128,8,128]{2,1,0:T(8,128)S(1)}, f32[128,8,128]{2,1,0:T(8,128)}, u32[]{:S(2)}) %copy-start.1) | copy-done | bytes 524312
  1.8 0.0 copy-start.2
  1.8 0.7 copy-done.2
  2.5 0.0 copy-start.3
  2.5 0.7 copy-done.3
  3.1 2.2 %pack.1 = f32[16,17,8,128]{3,2,1,0:T(8,128)S(1)} custom-call(s32[128]{0:T(128)S(1)} %bitcast.1, s32[128]{0:T(128)S(1)} %copy-done.3, f32[128,8,128]{2,1,0:T(8,128)S(1)} %copy-done.1), custom_call_target="tpu_custom_call" | custom-call | tf_op jit(solution)/shard_map/pack/pallas_call | solution.py:242
  5.4 32.4 %all_to_all.5.box_ref = f32[16,17,8,128]{3,2,1,0:T(8,128)S(1)} all-to-all(f32[16,17,8,128]{3,2,1,0:T(8,128)S(1)} %pack.1), channel_id=1, replica_groups=mesh['groups'=2,'row'=16] {'row'}, dimensions={0} | all-to-all | bytes 2228224 | tf_op jit(solution)/shard_map/all_to_all | solution.py:251
  37.8 0.1 convert_element_type.8.tags_ref
  37.9 0.0 copy-done
  37.9 7.7 %merge.1.m_ref = f32[256,2048]{1,0:T(8,128)} custom-call(s32[256]{0:T(256)S(1)} %convert_element_type.8.tags_ref, f32[256,2048]{1,0:T(8,128)S(1)} %copy-done, f32[16,17,8,128]{3,2,1,0:T(8,128)S(1)} %all_to_all.5.box_ref), custom_call_target="tpu_custom_call" | custom-call | tf_op jit(solution)/shard_map/merge/pallas_call | solution.py:253
  45.6 53.9 %opening.1 = (f32[256,2048]{1,0:T(8,128)S(1)}, f32[256,2048]{1,0:T(8,128)S(1)}) custom-call(f32[256,2048]{1,0:T(8,128)} %merge.1.m_ref), custom_call_target="tpu_custom_call" | custom-call | tf_op jit(solution)/shard_map/opening/pallas_call | solution.py:262
  99.6 1.3 %copy.9 = f32[256,2048]{1,0:T(8,128)} copy(f32[256,2048]{1,0:T(8,128)S(1)} %get-tuple-element.11) | data formatting | bytes 4194304
  100.9 1.3 %copy.10 = f32[256,2048]{1,0:T(8,128)} copy(f32[256,2048]{1,0:T(8,128)S(1)} %get-tuple-element.12) | data formatting | bytes 4194304
  (1 shorter events, 0.0 us)
Async XLA Ops:
  0.6 37.3 %copy-start = (f32[256,2048]{1,0:T(8,128)S(1)}, f32[256,2048]{1,0:T(8,128)}, u32[]{:S(2)}) copy-start(f32[256,2048]{1,0:T(8,128)} %base_ref.1) | copy-start | bytes 6291460
  0.6 1.2 %copy-start.1 = (f32[128,8,128]{2,1,0:T(8,128)S(1)}, f32[128,8,128]{2,1,0:T(8,128)}, u32[]{:S(2)}) copy-start(f32[128,8,128]{2,1,0:T(8,128)} %strips_ref.1) | copy-start | bytes 1572868
  1.8 0.7 copy-start.2
  2.5 0.7 copy-start.3
